TPU v7x, 32 devices: a whole 2x2x4 slice. The times are simulated.
32 devices in a mesh: groups: 2 (over x), wide: 16 (over z, y, core).
Axes of the slice: x: 2, y: 2, z: 4, core: 2. Of those that a mesh axis runs over, the one named last changes fastest.
Arguments:
- queries: bfloat16 [64, 8192], P(('groups', 'wide')), parts along dimension 0, may hold values from -120 to 120
- key_cache_array: bfloat16 [64, 256, 512], P(('groups', 'wide')), parts along dimension 0, may hold values from -6.1 to 6.1
- value_cache_array: bfloat16 [64, 256, 512], P(('groups', 'wide')), parts along dimension 0, may hold values from -16 to 16
- fresh_keys: bfloat16 [64, 512], P(('groups', 'wide')), parts along dimension 0, may hold values from -6 to 6
- fresh_values: bfloat16 [64, 512], P(('groups', 'wide')), parts along dimension 0, may hold values from -16 to 16
- lengths: int32 [64], P(('groups', 'wide')), parts along dimension 0, may hold values from 1 to 256, 4096 in all
- resid: bfloat16 [64, 8192], P(('groups', 'wide')), parts along dimension 0, may hold values from -1.5 to 1.5
- gain: bfloat16 [8192], replicated, may hold values from 0.099609375 to 1.8984375
- gate_weight: bfloat16 [8192, 26624], P(None, 'wide'), may hold values from -0.0625 to 0.0625
- up_weight: bfloat16 [8192, 26624], P(None, 'wide'), may hold values from -0.0625 to 0.0625
- down_weight: bfloat16 [26624, 8192], P('wide'), may hold values from -0.0390625 to 0.0390625
Outputs:
- mixed: bfloat16 [64, 8192], P(('groups', 'wide')), parts along dimension 0
There are 2 independent parts, one for each index of `groups`. A program takes and returns all parts, laid end to end along the dimension named above; an argument that names none is the same for every part. Nothing has to cross between parts.
All inputs are finite; a program needn't handle non-finite values. No bound on the sum of `lengths` on one device may be relied on, other than what follows from the above.
Results may differ from a plain program's by a relative error of at most 0.0055.
Values may be sent and summed in bfloat16 or wider, within the bound.
A program may use at most 192 MiB of HBM per device.

v0:
```python
import math

import jax
import jax.numpy as jnp
from jax import lax
from jax.sharding import PartitionSpec as P

QUERY_HEADS = 64
KEY_VALUE_HEADS = 4
HEAD_SIZE = 128
CACHE_LENGTH = 256


NEG_FILL = -1e30


def attend_rows(queries, key_cache_array, value_cache_array, fresh_keys, fresh_values, lengths):
    count_of_rows = queries.shape[0]
    queries_per_group = QUERY_HEADS // KEY_VALUE_HEADS
    score_scale = 1.0 / math.sqrt(HEAD_SIZE)
    query_vector = queries.reshape(count_of_rows, KEY_VALUE_HEADS, queries_per_group, HEAD_SIZE)
    cached_key_rows = key_cache_array.reshape(
        count_of_rows, CACHE_LENGTH, KEY_VALUE_HEADS, HEAD_SIZE
    )
    cached_value_rows = value_cache_array.reshape(
        count_of_rows, CACHE_LENGTH, KEY_VALUE_HEADS, HEAD_SIZE
    )
    token_key = fresh_keys.reshape(count_of_rows, KEY_VALUE_HEADS, HEAD_SIZE)
    token_value = fresh_values.reshape(count_of_rows, KEY_VALUE_HEADS, HEAD_SIZE).astype(
        jnp.float32
    )
    own_score = (
        jnp.einsum("shgd,shd->shg", query_vector, token_key, preferred_element_type=jnp.float32)
        * score_scale
    )
    scores = (
        jnp.einsum(
            "shgd,slhd->shgl", query_vector, cached_key_rows, preferred_element_type=jnp.float32
        )
        * score_scale
    )
    inside = (lax.iota(jnp.int32, CACHE_LENGTH)[None, :] < lengths[:, None])[:, None, None, :]
    scores = jnp.where(inside, scores, NEG_FILL)
    row_max = jnp.maximum(jnp.max(scores, axis=-1), own_score)
    weights = jnp.where(inside, jnp.exp(scores - row_max[..., None]), 0.0)
    own_weight = jnp.exp(own_score - row_max)
    totals = jnp.sum(weights, axis=-1) + own_weight
    own_low = lax.optimization_barrier(own_weight.astype(jnp.bfloat16)).astype(jnp.float32)
    heads_out = jnp.einsum(
        "shgl,slhd->shgd",
        weights.astype(jnp.bfloat16),
        cached_value_rows,
        preferred_element_type=jnp.float32,
    )
    heads_out = heads_out + own_low[..., None] * token_value[:, :, None, :]
    return (heads_out / totals[..., None]).reshape(count_of_rows, QUERY_HEADS * HEAD_SIZE)


def layer_rows(
    queries,
    key_cache_array,
    value_cache_array,
    fresh_keys,
    fresh_values,
    lengths,
    resid,
    gain,
    gate_weight,
    up_weight,
    down_weight,
):
    attended = attend_rows(
        queries, key_cache_array, value_cache_array, fresh_keys, fresh_values, lengths
    )
    stream = resid.astype(jnp.float32) + attended
    normed = (
        stream
        * lax.rsqrt(jnp.mean(stream * stream, axis=-1, keepdims=True) + 1e-05)
        * gain.astype(jnp.float32)
    ).astype(jnp.bfloat16)
    row_piece = lax.all_gather(normed, "wide", axis=0, tiled=True)
    gate = jnp.dot(row_piece, gate_weight, preferred_element_type=jnp.float32)
    up_part = jnp.dot(row_piece, up_weight, preferred_element_type=jnp.float32)
    hidden_all = (jax.nn.silu(gate) * up_part).astype(jnp.bfloat16)
    down_part = lax.psum_scatter(
        jnp.dot(hidden_all, down_weight, preferred_element_type=jnp.float32),
        "wide",
        scatter_dimension=0,
        tiled=True,
    )
    return (stream + down_part).astype(jnp.bfloat16)


def body(
    queries,
    key_cache_array,
    value_cache_array,
    fresh_keys,
    fresh_values,
    lengths,
    resid,
    gain,
    gate_weight,
    up_weight,
    down_weight,
):
    return layer_rows(
        queries,
        key_cache_array,
        value_cache_array,
        fresh_keys,
        fresh_values,
        lengths,
        resid,
        gain,
        gate_weight,
        up_weight,
        down_weight,
    )


def solution(mesh):
    return jax.shard_map(
        body,
        mesh=mesh,
        in_specs=(
            P(("groups", "wide"), None),
            P(("groups", "wide"), None, None),
            P(("groups", "wide"), None, None),
            P(("groups", "wide"), None),
            P(("groups", "wide"), None),
            P(("groups", "wide")),
            P(("groups", "wide"), None),
            P(),
            P(None, "wide"),
            P(None, "wide"),
            P("wide", None),
        ),
        out_specs=P(("groups", "wide"), None),
        check_vma=False,
    )
```

profile of v0, /device:TPU:0, one launch (start us, length us, event | category | flops | bytes accessed | tf_op | source)
XLA Modules:
  0.0 170.5 jit_solution(7541692568580045441)
XLA Ops:
  6.5 0.0 copy-start
  6.5 0.0 all-reduce.3.cloned.1.call-start
  6.5 0.8 iota_compare_fusion
  7.3 0.8 copy.20
  8.1 0.7 reshape.63
  8.8 0.1 fusion.27
  8.9 0.0 copy-done
  8.9 0.3 fusion.26
  9.3 0.2 fusion.13
  9.5 0.7 reshape.57
  10.2 1.3 fusion.3
  11.5 1.0 multiply_reduce_fusion
  12.4 0.7 convert_element_type.40
  13.1 0.9 fusion.21
  14.0 24.6 %all-gather = bf16[16,2,8192]{2,1,0:T(2,128)(2,1)S(1)} all-gather(bf16[1,2,8192]{2,1,0:T(2,128)(2,1)S(1)} %fusion.21), channel_id=1, replica_groups=mesh['groups'=2,'wide'=16] {'wide'}, dimensions={0}, use_global_device_ids=true | all-gather | bytes 557056 | tf_op jit(solution)/shard_map/all_gather | solution.py:81
  38.6 0.2 reshape.59
  38.8 11.1 %fusion.28 = f32[32,1664]{1,0:T(8,128)S(1)} fusion(bf16[32,8192]{1,0:T(8,128)(2,1)S(1)} %reshape.59, bf16[8192,1664]{1,0:T(8,128)(2,1)} %param.19), kind=kOutput, calls=%fused_computation.39 | convolution fusion | flops 872415232 | bytes 28000256 | tf_op jit(solution)/shard_map/dot_general | solution.py:82
  49.9 0.0 copy-start.2
  49.9 0.0 copy-start.1
  49.9 21.5 %fusion.1 = f32[32,8192]{1,0:T(8,128)} fusion(bf16[1664,8192]{1,0:T(8,128)(2,1)} %param.21, bf16[32,8192]{1,0:T(8,128)(2,1)S(1)} %reshape.59, bf16[8192,1664]{1,0:T(8,128)(2,1)} %param.20, f32[32,1664]{1,0:T(8,128)S(1)} %fusion.28), kind=kOutput, calls=%fused_computation.2 | convolution fusion | flops 1745149952 | bytes 56311808 | tf_op jit(solution)/shard_map/dot_general | solution.py:86
  71.4 0.0 all-reduce.3.cloned.1.call-update
  71.4 0.0 copy-done.2
  71.5 0.6 dynamic-slice
  72.7 89.3 %all-reduce.3.cloned.1.call-done = f32[32,8192]{1,0:T(8,128)} async-done(((f32[32,8192]{1,0:T(8,128)}), f32[32,8192]{1,0:T(8,128)}) %all-reduce.3.cloned.1.call-update) | async-done | bytes 1048592
  162.0 0.0 copy-done.1
  162.0 1.6 fusion.17
  (4 shorter events, 0.0 us)
Async XLA Ops:
  6.5 2.4 %copy-start = (bf16[2,256,512]{2,1,0:T(8,128)(2,1)S(1)}, bf16[2,256,512]{2,1,0:T(8,128)(2,1)}, u32[]{:S(2)}) copy-start(bf16[2,256,512]{2,1,0:T(8,128)(2,1)} %param.12) | copy-start | bytes 1572868
  6.5 155.5 %all-reduce.3.cloned.1.call-start = ((), (), s32[]{:S(2)}) async-start(), calls=%async_computation | async-start | bytes 2097152
  49.9 21.5 %copy-start.2 = (u32[32]{0:T(128)S(1)}, u32[32]{0:T(128)}, u32[]{:S(2)}) copy-start(u32[32]{0:T(128)} %constant.26) | copy-start | bytes 388
  49.9 112.1 %copy-start.1 = (bf16[2,8192]{1,0:T(2,128)(2,1)S(1)}, bf16[2,8192]{1,0:T(2,128)(2,1)}, u32[]{:S(2)}) copy-start(bf16[2,8192]{1,0:T(2,128)(2,1)} %param.17) | copy-start | bytes 98308
Sparse Core Ops, SparseCore 0:
  71.6 90.4 all-reduce.2
where the time goes:
time: 171 us; the launch traced here: 170 us
  waiting for transfers between devices  89.3 us (52%)
  matrix products  34.3 us (20%)
  blocking collectives  24.6 us (14%)
  between operations  14.1 us (8%)
  other arithmetic  5.18 us (3%)
  local copies, waits for them, and re-layouts  2.95 us (2%)
    unnamed x2, waiting for transfers between devices  89.3 us
    all_gather x1, blocking collectives, layer_rows(): row_piece = lax.all_gather(normed, 'wide', axis=0, tiled=True)  24.6 us
    dot_general x1, matrix products, layer_rows(): jnp.dot(hidden_all, down_weight, preferred_element_type=jnp.float32)  21.5 us
    dot_general x1, matrix products, layer_rows(): gate = jnp.dot(row_piece, gate_weight, preferred_element_type=jnp.float32)  11.1 us
  transfers between devices with their start and end apart: 1, of which 1 were waited for; matrix products, arithmetic and copies ran while one was open for 0% of the time, Pallas kernels for 0%

commit v1 on v0

v1 whole, which is shorter than its diff:
```python
import functools
import math

import jax
import jax.numpy as jnp
from jax import lax
from jax.experimental import pallas as pl
from jax.experimental.pallas import tpu as pltpu
from jax.sharding import PartitionSpec as P

HEAD_SIZE = 128
NEG_FILL = -1e30
MESH = pl.DeviceIdType.MESH
MIB = 1024 * 1024

CHUNK = 512
GATHER_PIECES = 4
SUM_PIECES = 4


def kernel(
    n,
    gather_pieces,
    sum_pieces,
    lengths,
    queries,
    keys,
    values,
    fresh_keys,
    fresh_values,
    resid,
    gain,
    gate_w,
    up_w,
    down_w,
    out,
    q_in,
    k_in,
    v_in,
    fk_in,
    fv_in,
    r_in,
    g_in,
    q_heads,
    stream,
    gate_buf,
    up_buf,
    down_buf,
    gathered,
    gate_acc,
    up_acc,
    hidden,
    part32,
    part16,
    from_pair,
    to_chips,
    from_chips,
    in_sem,
    gate_sem,
    up_sem,
    down_sem,
    ag_send,
    ag_recv,
    fw_send,
    fw_recv,
    pair_send,
    pair_recv,
    rs_send,
    rs_recv,
):
    rows, width = queries.shape
    heads = width // HEAD_SIZE
    kv_heads = keys.shape[2] // HEAD_SIZE
    per_kv = heads // kv_heads
    length = keys.shape[1]
    chips = n // 2
    chunks = width // CHUNK
    gu_slots = gate_buf.shape[0]
    dn_slots = down_buf.shape[0]
    per_gather = chunks // gather_pieces
    per_sum = chunks // sum_pieces
    half = rows * chips

    me = lax.axis_index("wide")
    chip = me // 2
    core = lax.rem(me, 2)
    pair = me + 1 - 2 * core

    def gate_copy(t):
        slot = lax.rem(t, gu_slots)
        src = gate_w.at[pl.ds(pl.multiple_of(t * CHUNK, CHUNK), CHUNK)]
        return pltpu.make_async_copy(src, gate_buf.at[slot], gate_sem.at[slot])

    def up_copy(t):
        slot = lax.rem(t, gu_slots)
        src = up_w.at[pl.ds(pl.multiple_of(t * CHUNK, CHUNK), CHUNK)]
        return pltpu.make_async_copy(src, up_buf.at[slot], up_sem.at[slot])

    def down_copy(t):
        slot = lax.rem(t, dn_slots)
        src = down_w.at[:, pl.ds(pl.multiple_of(t * CHUNK, CHUNK), CHUNK)]
        return pltpu.make_async_copy(src, down_buf.at[slot], down_sem.at[slot])

    small = [
        pltpu.make_async_copy(src, dst, in_sem.at[i])
        for i, (src, dst) in enumerate(
            [
                (queries, q_in),
                (keys, k_in),
                (fresh_keys, fk_in),
                (values, v_in),
                (fresh_values, fv_in),
                (resid, r_in),
                (gain, g_in),
            ]
        )
    ]
    for copy in small:
        copy.start()

    barrier = pltpu.get_barrier_semaphore()
    pl.semaphore_signal(barrier, inc=1, device_id={"wide": pair}, device_id_type=MESH)

    @pl.loop(1, chips)
    def _(d):
        pl.semaphore_signal(
            barrier,
            inc=1,
            device_id={"wide": 2 * lax.rem(chip + d, chips) + core},
            device_id_type=MESH,
        )

    @pl.loop(0, gu_slots)
    def _(t):
        gate_copy(t).start()
        up_copy(t).start()

    gate_acc[...] = jnp.zeros_like(gate_acc)
    up_acc[...] = jnp.zeros_like(up_acc)

    for copy in small:
        copy.wait()
    scale = 1.0 / math.sqrt(HEAD_SIZE)
    q32 = q_in[...].astype(jnp.float32)
    for r in range(rows):
        for h in range(heads):
            q_heads[r * heads + h : r * heads + h + 1, :] = q32[
                r : r + 1, h * HEAD_SIZE : (h + 1) * HEAD_SIZE
            ]
    position = lax.broadcasted_iota(jnp.int32, (per_kv, length), 1)
    fk32 = fk_in[...].astype(jnp.float32)
    fv32 = fv_in[...].astype(jnp.float32)
    for r in range(rows):
        inside = position < lengths[r]
        for k in range(kv_heads):
            lanes = slice(k * HEAD_SIZE, (k + 1) * HEAD_SIZE)
            first = r * heads + k * per_kv
            q = q_heads[first : first + per_kv, :]
            own_score = jnp.sum(q * fk32[r : r + 1, lanes], axis=-1, keepdims=True) * scale
            scores = (
                lax.dot_general(
                    q.astype(jnp.bfloat16),
                    k_in[r, :, lanes],
                    (((1,), (1,)), ((), ())),
                    preferred_element_type=jnp.float32,
                )
                * scale
            )
            scores = jnp.where(inside, scores, NEG_FILL)
            row_max = jnp.maximum(jnp.max(scores, axis=-1, keepdims=True), own_score)
            weights = jnp.where(inside, jnp.exp(scores - row_max), 0.0)
            own_weight = jnp.exp(own_score - row_max)
            totals = jnp.sum(weights, axis=-1, keepdims=True) + own_weight
            own_low = own_weight.astype(jnp.bfloat16).astype(jnp.float32)
            attended = jnp.dot(
                weights.astype(jnp.bfloat16),
                v_in[r, :, lanes],
                preferred_element_type=jnp.float32,
            )
            attended = (attended + own_low * fv32[r : r + 1, lanes]) / totals
            for i in range(per_kv):
                col = (k * per_kv + i) * HEAD_SIZE
                stream[r : r + 1, col : col + HEAD_SIZE] = attended[i : i + 1, :]

    total = stream[...] + r_in[...].astype(jnp.float32)
    stream[...] = total
    mean = jnp.sum(total * total, axis=-1, keepdims=True) * (1.0 / width)
    normed = (total * lax.rsqrt(mean + 1e-05) * g_in[...].astype(jnp.float32)).astype(jnp.bfloat16)

    my_slot = core * chips + chip
    piece = width // gather_pieces
    for q in range(gather_pieces):
        gathered[q, my_slot] = normed[:, q * piece : (q + 1) * piece]

    def ag_copy(q, d):
        return pltpu.make_async_remote_copy(
            gathered.at[q, my_slot],
            gathered.at[q, my_slot],
            ag_send.at[q, d],
            ag_recv.at[q, d],
            device_id={"wide": 2 * lax.rem(chip + d, chips) + core},
            device_id_type=MESH,
        )

    def fw_copy(q, d):
        slot = core * chips + lax.rem(chip - d + chips, chips)
        return pltpu.make_async_remote_copy(
            gathered.at[q, slot],
            gathered.at[q, slot],
            fw_send.at[q, d],
            fw_recv.at[q, d],
            device_id={"wide": pair},
            device_id_type=MESH,
        )

    pl.semaphore_wait(barrier, chips)

    @pl.loop(0, gather_pieces)
    def _(q):
        fw_copy(q, 0).start()

        @pl.loop(1, chips)
        def _(d):
            ag_copy(q, d).start()

    def forward(q):
        @pl.loop(1, chips)
        def _(d):
            ag_copy(q, d).wait_recv()
            fw_copy(q, d).start()

    forward(0)

    @pl.loop(0, chunks)
    def _(t):
        q = t // per_gather
        j = lax.rem(t, per_gather)

        @pl.when(j == 0)
        def _():
            @pl.loop(0, chips)
            def _(d):
                fw_copy(q, d).wait_recv()

        @pl.when(jnp.logical_and(j == min(1, per_gather - 1), q + 1 < gather_pieces))
        def _():
            forward(q + 1)

        cols = pl.ds(pl.multiple_of(j * CHUNK, CHUNK), CHUNK)
        x = gathered[q, :, :, cols].reshape(rows * n, CHUNK)
        slot = lax.rem(t, gu_slots)
        gate_copy(t).wait()
        gate_acc[...] += jnp.dot(x, gate_buf[slot], preferred_element_type=jnp.float32)
        up_copy(t).wait()
        up_acc[...] += jnp.dot(x, up_buf[slot], preferred_element_type=jnp.float32)

        @pl.when(t + gu_slots < chunks)
        def _():
            gate_copy(t + gu_slots).start()
            up_copy(t + gu_slots).start()

        later = 2 * (t + gu_slots - chunks)

        @pl.when(jnp.logical_and(later >= 0, later < dn_slots))
        def _():
            down_copy(later).start()
            down_copy(later + 1).start()

    gate = gate_acc[...]
    hidden[...] = (gate / (1.0 + jnp.exp(-gate)) * up_acc[...]).astype(jnp.bfloat16)

    mine = pl.multiple_of(core * half, half)
    other = pl.multiple_of((1 - core) * half, half)

    def pair_copy(p):
        return pltpu.make_async_remote_copy(
            part16.at[p, pl.ds(other, half)],
            from_pair.at[p],
            pair_send.at[p],
            pair_recv.at[p],
            device_id={"wide": pair},
            device_id_type=MESH,
        )

    def rs_copy(p, d):
        dest = lax.rem(chip + d, chips)
        return pltpu.make_async_remote_copy(
            to_chips.at[p, dest],
            from_chips.at[p, chip],
            rs_send.at[p, d],
            rs_recv.at[p, d],
            device_id={"wide": 2 * dest + core},
            device_id_type=MESH,
        )

    def reduce_pair(p):
        pair_copy(p).wait_recv()
        both = part32[p, pl.ds(mine, half)] + from_pair[p].astype(jnp.float32)
        to_chips[p] = both.astype(jnp.bfloat16).reshape(to_chips.shape[1:])

        @pl.loop(1, chips)
        def _(d):
            rs_copy(p, d).start()

        from_chips[p, chip] = to_chips[p, chip]

    @pl.loop(0, chunks)
    def _(t):
        p = t // per_sum
        j = lax.rem(t, per_sum)
        cols = pl.ds(pl.multiple_of(j * CHUNK, CHUNK), CHUNK)
        down_copy(t).wait()
        part = jnp.dot(
            hidden[...], down_buf[lax.rem(t, dn_slots)], preferred_element_type=jnp.float32
        )
        part32[p, :, cols] = part
        part16[p, :, cols] = part.astype(jnp.bfloat16)

        @pl.when(t + dn_slots < chunks)
        def _():
            down_copy(t + dn_slots).start()

        @pl.when(j == per_sum - 1)
        def _():
            pair_copy(p).start()

        @pl.when(jnp.logical_and(j == min(1, per_sum - 1), p > 0))
        def _():
            reduce_pair(p - 1)

    reduce_pair(sum_pieces - 1)

    columns = width // sum_pieces
    for p in range(sum_pieces):

        @pl.loop(1, chips)
        def _(d):
            rs_copy(p, d).wait_recv()

        span = slice(p * columns, (p + 1) * columns)
        summed = jnp.sum(from_chips[p].astype(jnp.float32), axis=0)
        out[:, span] = (stream[:, span] + summed).astype(out.dtype)

    @pl.loop(0, gather_pieces)
    def _(q):
        fw_copy(q, 0).wait_send()

        @pl.loop(1, chips)
        def _(d):
            ag_copy(q, d).wait_send()
            fw_copy(q, d).wait_send()

    @pl.loop(0, sum_pieces)
    def _(p):
        pair_copy(p).wait_send()

        @pl.loop(1, chips)
        def _(d):
            rs_copy(p, d).wait_send()


def body(
    queries,
    key_cache_array,
    value_cache_array,
    fresh_keys,
    fresh_values,
    lengths,
    resid,
    gain,
    gate_weight,
    up_weight,
    down_weight,
    *,
    n,
):
    rows, width = queries.shape
    units = gate_weight.shape[1]
    chips = n // 2
    heads = width // HEAD_SIZE
    chunks = width // CHUNK
    gu_slots = min(12, chunks)
    dn_slots = min(8, chunks)
    gq, sp = GATHER_PIECES, SUM_PIECES
    bf, f32 = jnp.bfloat16, jnp.float32
    any_spec = pl.BlockSpec(memory_space=pl.ANY)
    weights_bytes = 2 * 3 * width * units
    return pl.pallas_call(
        functools.partial(kernel, n, gq, sp),
        out_shape=jax.ShapeDtypeStruct((rows, width), bf),
        in_specs=[pl.BlockSpec(memory_space=pltpu.SMEM)] + [any_spec] * 10,
        out_specs=pl.BlockSpec(memory_space=pltpu.VMEM),
        scratch_shapes=[
            pltpu.VMEM(queries.shape, bf),
            pltpu.VMEM(key_cache_array.shape, bf),
            pltpu.VMEM(value_cache_array.shape, bf),
            pltpu.VMEM(fresh_keys.shape, bf),
            pltpu.VMEM(fresh_values.shape, bf),
            pltpu.VMEM(resid.shape, bf),
            pltpu.VMEM((1, width), bf),
            pltpu.VMEM((rows * heads, HEAD_SIZE), f32),
            pltpu.VMEM((rows, width), f32),
            pltpu.VMEM((gu_slots, CHUNK, units), bf),
            pltpu.VMEM((gu_slots, CHUNK, units), bf),
            pltpu.VMEM((dn_slots, units, CHUNK), bf),
            pltpu.VMEM((gq, n, rows, width // gq), bf),
            pltpu.VMEM((n * rows, units), f32),
            pltpu.VMEM((n * rows, units), f32),
            pltpu.VMEM((n * rows, units), bf),
            pltpu.VMEM((sp, n * rows, width // sp), f32),
            pltpu.VMEM((sp, n * rows, width // sp), bf),
            pltpu.VMEM((sp, chips * rows, width // sp), bf),
            pltpu.VMEM((sp, chips, rows, width // sp), bf),
            pltpu.VMEM((sp, chips, rows, width // sp), bf),
            pltpu.SemaphoreType.DMA((7,)),
            pltpu.SemaphoreType.DMA((gu_slots,)),
            pltpu.SemaphoreType.DMA((gu_slots,)),
            pltpu.SemaphoreType.DMA((dn_slots,)),
            pltpu.SemaphoreType.DMA((gq, chips)),
            pltpu.SemaphoreType.DMA((gq, chips)),
            pltpu.SemaphoreType.DMA((gq, chips)),
            pltpu.SemaphoreType.DMA((gq, chips)),
            pltpu.SemaphoreType.DMA((sp,)),
            pltpu.SemaphoreType.DMA((sp,)),
            pltpu.SemaphoreType.DMA((sp, chips)),
            pltpu.SemaphoreType.DMA((sp, chips)),
        ],
        compiler_params=pltpu.CompilerParams(
            collective_id=0, has_side_effects=True, vmem_limit_bytes=60 * MIB
        ),
        cost_estimate=pl.CostEstimate(
            flops=2 * n * rows * weights_bytes // 2,
            bytes_accessed=weights_bytes,
            transcendentals=n * rows * units,
        ),
        name="decode_layer",
    )(
        lengths,
        queries,
        key_cache_array,
        value_cache_array,
        fresh_keys,
        fresh_values,
        resid,
        gain.reshape(1, width),
        gate_weight,
        up_weight,
        down_weight,
    )


def solution(mesh):
    rows = P(("groups", "wide"), None)
    cache = P(("groups", "wide"), None, None)
    return jax.shard_map(
        functools.partial(body, n=mesh.shape["wide"]),
        mesh=mesh,
        in_specs=(
            rows,
            cache,
            cache,
            rows,
            rows,
            P(("groups", "wide")),
            rows,
            P(),
            P(None, "wide"),
            P(None, "wide"),
            P("wide", None),
        ),
        out_specs=rows,
        check_vma=False,
    )
```

time: 171 us -> 45.3 us (0.26)
  waiting for transfers between devices: 89.3 us -> 0 us
  Pallas kernels: 0 us -> 42.3 us
  matrix products: 34.3 us -> 0 us
  blocking collectives: 24.6 us -> 0 us
  between operations: 14.1 us -> 0.01 us
  other arithmetic: 5.18 us -> 0 us
    unnamed x2 -> x0, waiting for transfers between devices: 89.3 us -> none
    pallas_call x0 -> x1, Pallas kernels: none -> 42.3 us  [body(): pl.pallas_call(functools.partial(kernel, n, gq, sp), out_shape=jax.ShapeD...]
    dot_general x5 -> x0, matrix products: 34.3 us -> none  [the longest x1 21.5 us: layer_rows(): jnp.dot(hidden_all, down_weight, preferred_element_type=jnp.float32)]
    all_gather x1 -> x0, blocking collectives: 24.6 us -> none  [layer_rows(): row_piece = lax.all_gather(normed, 'wide', axis=0, tiled=True)]
    convert_element_type x4 -> x0, other arithmetic: 2.38 us -> none  [the longest x1 1.64 us: layer_rows(): return (stream + down_part).astype(jnp.bfloat16)]
  transfers between devices with their start and end apart: 1 -> 0, of which waited for: 1 -> 0; matrix products, arithmetic and copies ran while one was open for 0% -> 0% of each run, Pallas kernels for 0% -> 0%
where the time goes in v1:
time: 45.3 us; the launch traced here: 45.1 us
  Pallas kernels  42.3 us (93%)
  local copies, waits for them, and re-layouts  2.75 us (6%)
    pallas_call x1, Pallas kernels, body(): pl.pallas_call(functools.partial(kernel, n, gq, sp), out_shape=jax.ShapeD...  42.3 us
    unnamed x1, local copies, waits for them, and re-layouts  1.4 us
    reshape x1, local copies, waits for them, and re-layouts, body(): gain.reshape(1, width)  1.35 us

profile of v1, /device:TPU:0, one launch (start us, length us, event | category | flops | bytes accessed | tf_op | source)
XLA Modules:
  0.0 45.1 jit_solution(15376063766903677125)
XLA Ops:
  0.0 1.3 %reshape.3.gain = bf16[1,8192]{1,0:T(2,128)(2,1)} reshape(bf16[8192]{0:T(1024)(128)(2,1)} %param.18) | data formatting | bytes 32768 | tf_op jit(solution)/shard_map/reshape | solution.py:445
  1.4 42.3 %decode_layer.1 = bf16[2,8192]{1,0:T(2,128)(2,1)} custom-call(s32[2]{0:T(128)} %lengths.1, bf16[2,8192]{1,0:T(2,128)(2,1)} %queries.1, bf16[2,256,512]{2,1,0:T(8,128)(2,1)} %keys.1, bf16[2,256,512]{2,1,0:T(8,128)(2,1)} %values.1, bf16[2,512]{1,0:T(2,128)(2,1)} %fresh_keys.1, bf16[2,512]{1,0:T(2,128)(2,1)} %fresh_values.1, bf16[2,8192]{1,0:T(2,128)(2,1)} %resid.1, ...), custom_call_target="tpu_custom_call" | custom-call | flops 2617245696 | bytes 81788928 | tf_op jit(solution)/shard_map/decode_layer/pallas_call | solution.py:388
  43.7 1.4 %copy.13 = bf16[2,8192]{1,0:T(2,128)(2,1)} copy(bf16[2,8192]{1,0:T(2,128)(2,1)} %decode_layer.1) | data formatting | bytes 65536

commit v2 on v1

v2 whole, which is shorter than its diff:
```python
import functools
import math

import jax
import jax.numpy as jnp
from jax import lax
from jax.experimental import pallas as pl
from jax.experimental.pallas import tpu as pltpu
from jax.sharding import PartitionSpec as P

HEAD_SIZE = 128
NEG_FILL = -1e30
MESH = pl.DeviceIdType.MESH
MIB = 1024 * 1024

CHUNK = 512
GATHER_PIECES = 4
SUM_PIECES = 4


def kernel(
    n,
    groups,
    gather_pieces,
    sum_pieces,
    lengths,
    queries,
    keys,
    values,
    fresh_keys,
    fresh_values,
    resid,
    gain,
    gate_w,
    up_w,
    down_w,
    out,
    q_in,
    k_in,
    v_in,
    fk_in,
    fv_in,
    r_in,
    g_in,
    q_heads,
    stream,
    gate_buf,
    up_buf,
    down_buf,
    gathered,
    gate_acc,
    up_acc,
    hidden,
    part32,
    part16,
    from_pair,
    from_x,
    to_chips,
    from_chips,
    in_sem,
    gate_sem,
    up_sem,
    down_sem,
    ag_send,
    ag_recv,
    fw_send,
    fw_recv,
    x_send,
    x_recv,
    fx_send,
    fx_recv,
    pair_send,
    pair_recv,
    px_send,
    px_recv,
    rs_send,
    rs_recv,
):
    rows, width = queries.shape
    heads = width // HEAD_SIZE
    kv_heads = keys.shape[2] // HEAD_SIZE
    per_kv = heads // kv_heads
    length = keys.shape[1]
    chips = n // 2
    chunks = width // CHUNK
    window = gate_buf.shape[2]
    units = gate_w.shape[1]
    per_gather = chunks // gather_pieces
    per_sum = chunks // sum_pieces
    group_rows = rows * chips
    half = groups * group_rows

    group = lax.axis_index("groups")
    me = lax.axis_index("wide")
    chip = me // 2
    core = lax.rem(me, 2)
    pair = me + 1 - 2 * core
    if units == window:
        rows_from, cols_from = pl.ds(0, units), pl.ds(0, units)
    else:
        start = pl.multiple_of(group * (units - window), 128)
        rows_from = cols_from = pl.ds(start, window)

    def gate_copy(t):
        src = gate_w.at[pl.ds(pl.multiple_of(t * CHUNK, CHUNK), CHUNK), cols_from]
        return pltpu.make_async_copy(src, gate_buf.at[t], gate_sem.at[t])

    def up_copy(t):
        src = up_w.at[pl.ds(pl.multiple_of(t * CHUNK, CHUNK), CHUNK), cols_from]
        return pltpu.make_async_copy(src, up_buf.at[t], up_sem.at[t])

    def down_copy(t):
        src = down_w.at[rows_from, pl.ds(pl.multiple_of(t * CHUNK, CHUNK), CHUNK)]
        return pltpu.make_async_copy(src, down_buf.at[t], down_sem.at[t])

    small = [
        pltpu.make_async_copy(src, dst, in_sem.at[i])
        for i, (src, dst) in enumerate(
            [
                (queries, q_in),
                (keys, k_in),
                (fresh_keys, fk_in),
                (values, v_in),
                (fresh_values, fv_in),
                (resid, r_in),
                (gain, g_in),
            ]
        )
    ]
    for copy in small:
        copy.start()

    barrier = pltpu.get_barrier_semaphore()
    pl.semaphore_signal(barrier, inc=1, device_id={"wide": pair}, device_id_type=MESH)
    pl.semaphore_signal(
        barrier, inc=1, device_id={"groups": 1 - group}, device_id_type=MESH
    )

    @pl.loop(1, chips, unroll=chips <= 8)
    def _(d):
        pl.semaphore_signal(
            barrier,
            inc=1,
            device_id={"wide": 2 * lax.rem(chip + d, chips) + core},
            device_id_type=MESH,
        )

    @pl.loop(0, chunks)
    def _(t):
        gate_copy(t).start()
        up_copy(t).start()

    @pl.loop(0, chunks)
    def _(t):
        down_copy(t).start()

    gate_acc[...] = jnp.zeros_like(gate_acc)
    up_acc[...] = jnp.zeros_like(up_acc)

    for copy in small:
        copy.wait()
    scale = 1.0 / math.sqrt(HEAD_SIZE)
    q32 = q_in[...].astype(jnp.float32)
    for r in range(rows):
        for h in range(heads):
            q_heads[r * heads + h : r * heads + h + 1, :] = q32[
                r : r + 1, h * HEAD_SIZE : (h + 1) * HEAD_SIZE
            ]
    position = lax.broadcasted_iota(jnp.int32, (per_kv, length), 1)
    fk32 = fk_in[...].astype(jnp.float32)
    fv32 = fv_in[...].astype(jnp.float32)
    for r in range(rows):
        inside = position < lengths[r]
        for k in range(kv_heads):
            lanes = slice(k * HEAD_SIZE, (k + 1) * HEAD_SIZE)
            first = r * heads + k * per_kv
            q = q_heads[first : first + per_kv, :]
            own_score = jnp.sum(q * fk32[r : r + 1, lanes], axis=-1, keepdims=True) * scale
            scores = (
                lax.dot_general(
                    q.astype(jnp.bfloat16),
                    k_in[r, :, lanes],
                    (((1,), (1,)), ((), ())),
                    preferred_element_type=jnp.float32,
                )
                * scale
            )
            scores = jnp.where(inside, scores, NEG_FILL)
            row_max = jnp.maximum(jnp.max(scores, axis=-1, keepdims=True), own_score)
            weights = jnp.where(inside, jnp.exp(scores - row_max), 0.0)
            own_weight = jnp.exp(own_score - row_max)
            totals = jnp.sum(weights, axis=-1, keepdims=True) + own_weight
            own_low = own_weight.astype(jnp.bfloat16).astype(jnp.float32)
            attended = jnp.dot(
                weights.astype(jnp.bfloat16),
                v_in[r, :, lanes],
                preferred_element_type=jnp.float32,
            )
            attended = (attended + own_low * fv32[r : r + 1, lanes]) / totals
            for i in range(per_kv):
                col = (k * per_kv + i) * HEAD_SIZE
                stream[r : r + 1, col : col + HEAD_SIZE] = attended[i : i + 1, :]

    total = stream[...] + r_in[...].astype(jnp.float32)
    stream[...] = total
    mean = jnp.sum(total * total, axis=-1, keepdims=True) * (1.0 / width)
    normed = (total * lax.rsqrt(mean + 1e-05) * g_in[...].astype(jnp.float32).reshape(1, width)).astype(jnp.bfloat16)

    own_slots = (core * groups + group) * chips
    x_slots = (core * groups + 1 - group) * chips
    piece = width // gather_pieces
    for q in range(gather_pieces):
        gathered[q, own_slots + chip] = normed[:, q * piece : (q + 1) * piece]

    def send(q, slot, send_sem, recv_sem, device):
        return pltpu.make_async_remote_copy(
            gathered.at[q, slot],
            gathered.at[q, slot],
            send_sem,
            recv_sem,
            device_id=device,
            device_id_type=MESH,
        )

    def ag_copy(q, d):
        device = {"wide": 2 * lax.rem(chip + d, chips) + core}
        return send(q, own_slots + chip, ag_send.at[q, d], ag_recv.at[q, d], device)

    def x_copy(q):
        return send(
            q, pl.ds(own_slots, chips), x_send.at[q], x_recv.at[q], {"groups": 1 - group}
        )

    def fw_copy(q):
        return send(q, pl.ds(own_slots, chips), fw_send.at[q], fw_recv.at[q], {"wide": pair})

    def fx_copy(q):
        return send(q, pl.ds(x_slots, chips), fx_send.at[q], fx_recv.at[q], {"wide": pair})

    pl.semaphore_wait(barrier, chips + 1)

    @pl.loop(0, gather_pieces)
    def _(q):
        @pl.loop(1, chips, unroll=chips <= 8)
        def _(d):
            ag_copy(q, d).start()

    def forward(q):
        @pl.loop(1, chips, unroll=chips <= 8)
        def _(d):
            ag_copy(q, d).wait_recv()

        x_copy(q).start()
        fw_copy(q).start()

    def forward_x(q):
        x_copy(q).wait_recv()
        fx_copy(q).start()

    forward(0)
    if gather_pieces > 1:
        forward(1)
    forward_x(0)
    if gather_pieces > 2:
        forward(2)

    @pl.loop(0, chunks, unroll=4)
    def _(t):
        q = t // per_gather
        j = lax.rem(t, per_gather)

        @pl.when(j == 0)
        def _():
            fw_copy(q).wait_recv()
            fx_copy(q).wait_recv()

        @pl.when(jnp.logical_and(j == per_gather // 2, q + 1 < gather_pieces))
        def _():
            forward_x(q + 1)

            @pl.when(q + 3 < gather_pieces)
            def _():
                forward(q + 3)

        cols = pl.ds(pl.multiple_of(j * CHUNK, CHUNK), CHUNK)
        x = gathered[q, :, :, cols].reshape(rows * n * groups, CHUNK)
        gate_copy(t).wait()
        gate_acc[...] += jnp.dot(x, gate_buf[t], preferred_element_type=jnp.float32)
        up_copy(t).wait()
        up_acc[...] += jnp.dot(x, up_buf[t], preferred_element_type=jnp.float32)

    gate = gate_acc[...]
    unit = lax.broadcasted_iota(jnp.int32, gate.shape, 1) + group * (units - window)
    act = jnp.where(unit >= group * window, gate / (1.0 + jnp.exp(-gate)) * up_acc[...], 0.0)
    hidden[...] = act.astype(jnp.bfloat16)

    mine = pl.multiple_of(core * half, half)
    other = pl.multiple_of((1 - core) * half, half)
    own_rows = pl.ds(pl.multiple_of(mine + group * group_rows, group_rows), group_rows)
    x_rows = pl.ds(pl.multiple_of(mine + (1 - group) * group_rows, group_rows), group_rows)

    def pair_copy(p):
        return pltpu.make_async_remote_copy(
            part16.at[p, pl.ds(other, half)],
            from_pair.at[p],
            pair_send.at[p],
            pair_recv.at[p],
            device_id={"wide": pair},
            device_id_type=MESH,
        )

    def px_copy(p):
        return pltpu.make_async_remote_copy(
            part16.at[p, x_rows],
            from_x.at[p],
            px_send.at[p],
            px_recv.at[p],
            device_id={"groups": 1 - group},
            device_id_type=MESH,
        )

    def rs_copy(p, d):
        dest = lax.rem(chip + d, chips)
        return pltpu.make_async_remote_copy(
            to_chips.at[p, dest],
            from_chips.at[p, chip],
            rs_send.at[p, d],
            rs_recv.at[p, d],
            device_id={"wide": 2 * dest + core},
            device_id_type=MESH,
        )

    def reduce_pair(p):
        pair_copy(p).wait_recv()
        here = pl.ds(pl.multiple_of((1 - group) * group_rows, group_rows), group_rows)
        both = part32[p, x_rows] + from_pair[p, here].astype(jnp.float32)
        part16[p, x_rows] = both.astype(jnp.bfloat16)
        px_copy(p).start()
        here = pl.ds(pl.multiple_of(group * group_rows, group_rows), group_rows)
        part32[p, own_rows] += from_pair[p, here].astype(jnp.float32)

    def reduce_groups(p):
        px_copy(p).wait_recv()
        both = part32[p, own_rows] + from_x[p].astype(jnp.float32)
        to_chips[p] = both.astype(jnp.bfloat16).reshape(to_chips.shape[1:])

        @pl.loop(1, chips, unroll=chips <= 8)
        def _(d):
            rs_copy(p, d).start()

        from_chips[p, chip] = to_chips[p, chip]

    @pl.loop(0, chunks, unroll=4)
    def _(t):
        p = t // per_sum
        j = lax.rem(t, per_sum)
        cols = pl.ds(pl.multiple_of(j * CHUNK, CHUNK), CHUNK)
        down_copy(t).wait()
        part = jnp.dot(hidden[...], down_buf[t], preferred_element_type=jnp.float32)
        part32[p, :, cols] = part
        part16[p, :, cols] = part.astype(jnp.bfloat16)

        @pl.when(j == per_sum - 1)
        def _():
            pair_copy(p).start()

            @pl.when(p >= 1)
            def _():
                reduce_pair(p - 1)

    reduce_pair(sum_pieces - 1)

    @pl.loop(0, sum_pieces, unroll=True)
    def _(p):
        reduce_groups(p)

    columns = width // sum_pieces
    for p in range(sum_pieces):

        @pl.loop(1, chips, unroll=chips <= 8)
        def _(d):
            rs_copy(p, d).wait_recv()

        span = slice(p * columns, (p + 1) * columns)
        summed = jnp.sum(from_chips[p].astype(jnp.float32), axis=0)
        out[:, span] = (stream[:, span] + summed).astype(out.dtype)

    @pl.loop(0, gather_pieces)
    def _(q):
        x_copy(q).wait_send()
        fw_copy(q).wait_send()
        fx_copy(q).wait_send()

        @pl.loop(1, chips, unroll=chips <= 8)
        def _(d):
            ag_copy(q, d).wait_send()

    @pl.loop(0, sum_pieces, unroll=True)
    def _(p):
        pair_copy(p).wait_send()
        px_copy(p).wait_send()

        @pl.loop(1, chips, unroll=chips <= 8)
        def _(d):
            rs_copy(p, d).wait_send()


def body(
    queries,
    key_cache_array,
    value_cache_array,
    fresh_keys,
    fresh_values,
    lengths,
    resid,
    gain,
    gate_weight,
    up_weight,
    down_weight,
    *,
    n,
    groups,
):
    rows, width = queries.shape
    units = gate_weight.shape[1]
    chips = n // 2
    heads = width // HEAD_SIZE
    chunks = width // CHUNK
    window = units if units % 128 else -(-units // 256) * 128
    all_rows = n * groups * rows
    half = all_rows // 2
    gq, sp = GATHER_PIECES, SUM_PIECES
    bf, f32 = jnp.bfloat16, jnp.float32
    any_spec = pl.BlockSpec(memory_space=pl.ANY)
    weights_bytes = 2 * 3 * width * window
    return pl.pallas_call(
        functools.partial(kernel, n, groups, gq, sp),
        out_shape=jax.ShapeDtypeStruct((rows, width), bf),
        in_specs=[pl.BlockSpec(memory_space=pltpu.SMEM)] + [any_spec] * 10,
        out_specs=pl.BlockSpec(memory_space=pltpu.VMEM),
        scratch_shapes=[
            pltpu.VMEM(queries.shape, bf),
            pltpu.VMEM(key_cache_array.shape, bf),
            pltpu.VMEM(value_cache_array.shape, bf),
            pltpu.VMEM(fresh_keys.shape, bf),
            pltpu.VMEM(fresh_values.shape, bf),
            pltpu.VMEM(resid.shape, bf),
            pltpu.VMEM((width,), bf),
            pltpu.VMEM((rows * heads, HEAD_SIZE), f32),
            pltpu.VMEM((rows, width), f32),
            pltpu.VMEM((chunks, CHUNK, window), bf),
            pltpu.VMEM((chunks, CHUNK, window), bf),
            pltpu.VMEM((chunks, window, CHUNK), bf),
            pltpu.VMEM((gq, n * groups, rows, width // gq), bf),
            pltpu.VMEM((all_rows, window), f32),
            pltpu.VMEM((all_rows, window), f32),
            pltpu.VMEM((all_rows, window), bf),
            pltpu.VMEM((sp, all_rows, width // sp), f32),
            pltpu.VMEM((sp, all_rows, width // sp), bf),
            pltpu.VMEM((sp, half, width // sp), bf),
            pltpu.VMEM((sp, half // groups, width // sp), bf),
            pltpu.VMEM((sp, chips, rows, width // sp), bf),
            pltpu.VMEM((sp, chips, rows, width // sp), bf),
            pltpu.SemaphoreType.DMA((7,)),
            pltpu.SemaphoreType.DMA((chunks,)),
            pltpu.SemaphoreType.DMA((chunks,)),
            pltpu.SemaphoreType.DMA((chunks,)),
        ]
        + [pltpu.SemaphoreType.DMA((gq, chips))] * 2
        + [pltpu.SemaphoreType.DMA((gq,))] * 6
        + [pltpu.SemaphoreType.DMA((sp,))] * 4
        + [pltpu.SemaphoreType.DMA((sp, chips))] * 2,
        compiler_params=pltpu.CompilerParams(
            collective_id=0, has_side_effects=True, vmem_limit_bytes=60 * MIB
        ),
        cost_estimate=pl.CostEstimate(
            flops=all_rows * weights_bytes,
            bytes_accessed=weights_bytes,
            transcendentals=all_rows * window,
        ),
        name="decode_layer",
    )(
        lengths,
        queries,
        key_cache_array,
        value_cache_array,
        fresh_keys,
        fresh_values,
        resid,
        gain,
        gate_weight,
        up_weight,
        down_weight,
    )


def solution(mesh):
    rows = P(("groups", "wide"), None)
    cache = P(("groups", "wide"), None, None)
    return jax.shard_map(
        functools.partial(body, n=mesh.shape["wide"], groups=mesh.shape["groups"]),
        mesh=mesh,
        in_specs=(
            rows,
            cache,
            cache,
            rows,
            rows,
            P(("groups", "wide")),
            rows,
            P(),
            P(None, "wide"),
            P(None, "wide"),
            P("wide", None),
        ),
        out_specs=rows,
        check_vma=False,
    )
```

time: 45.3 us -> 44.5 us (0.982)
  local copies, waits for them, and re-layouts: 2.75 us -> 1.4 us
  Pallas kernels: 42.3 us -> 42.9 us
    reshape x1 -> x0, local copies, waits for them, and re-layouts: 1.35 us -> none  [body(): gain.reshape(1, width)]
    pallas_call x1, Pallas kernels: 42.3 us -> 42.9 us  [body(): pl.pallas_call(functools.partial(kernel, n, groups, gq, sp), out_shape=ja...]
where the time goes in v2:
time: 44.5 us; the launch traced here: 44.3 us
  Pallas kernels  42.9 us (96%)
  local copies, waits for them, and re-layouts  1.4 us (3%)
    pallas_call x1, Pallas kernels, body(): pl.pallas_call(functools.partial(kernel, n, groups, gq, sp), out_shape=ja...  42.9 us
    unnamed x1, local copies, waits for them, and re-layouts  1.4 us

profile of v2, /device:TPU:0, one launch (start us, length us, event | category | flops | bytes accessed | tf_op | source)
XLA Modules:
  0.0 44.3 jit_solution(1109672042840198901)
XLA Ops:
  0.0 42.9 %decode_layer.1 = bf16[2,8192]{1,0:T(2,128)(2,1)} custom-call(s32[2]{0:T(128)} %lengths.1, bf16[2,8192]{1,0:T(2,128)(2,1)} %queries.1, bf16[2,256,512]{2,1,0:T(8,128)(2,1)} %keys.1, bf16[2,256,512]{2,1,0:T(8,128)(2,1)} %values.1, bf16[2,512]{1,0:T(2,128)(2,1)} %fresh_keys.1, bf16[2,512]{1,0:T(2,128)(2,1)} %fresh_values.1, bf16[2,8192]{1,0:T(2,128)(2,1)} %resid.1, ...), custom_call_target="tpu_custom_call" | custom-call | flops 2818572288 | bytes 44040192 | tf_op jit(solution)/shard_map/decode_layer/pallas_call | solution.py:436
  42.9 1.4 %copy.13 = bf16[2,8192]{1,0:T(2,128)(2,1)} copy(bf16[2,8192]{1,0:T(2,128)(2,1)} %decode_layer.1) | data formatting | bytes 65536

commit v3 on v1

--- a/solution.py
+++ b/solution.py
@@ -121,7 +121,7 @@
     barrier = pltpu.get_barrier_semaphore()
     pl.semaphore_signal(barrier, inc=1, device_id={"wide": pair}, device_id_type=MESH)
 
-    @pl.loop(1, chips)
+    @pl.loop(1, chips, unroll=chips <= 8)
     def _(d):
         pl.semaphore_signal(
             barrier,
@@ -185,7 +185,7 @@
     total = stream[...] + r_in[...].astype(jnp.float32)
     stream[...] = total
     mean = jnp.sum(total * total, axis=-1, keepdims=True) * (1.0 / width)
-    normed = (total * lax.rsqrt(mean + 1e-05) * g_in[...].astype(jnp.float32)).astype(jnp.bfloat16)
+    normed = (total * lax.rsqrt(mean + 1e-05) * g_in[...].astype(jnp.float32).reshape(1, width)).astype(jnp.bfloat16)
 
     my_slot = core * chips + chip
     piece = width // gather_pieces
@@ -202,13 +202,13 @@
             device_id_type=MESH,
         )
 
-    def fw_copy(q, d):
-        slot = core * chips + lax.rem(chip - d + chips, chips)
+    def fw_copy(q):
+        block = gathered.at[q, pl.ds(core * chips, chips)]
         return pltpu.make_async_remote_copy(
-            gathered.at[q, slot],
-            gathered.at[q, slot],
-            fw_send.at[q, d],
-            fw_recv.at[q, d],
+            block,
+            block,
+            fw_send.at[q],
+            fw_recv.at[q],
             device_id={"wide": pair},
             device_id_type=MESH,
         )
@@ -217,30 +217,27 @@
 
     @pl.loop(0, gather_pieces)
     def _(q):
-        fw_copy(q, 0).start()
-
-        @pl.loop(1, chips)
+        @pl.loop(1, chips, unroll=chips <= 8)
         def _(d):
             ag_copy(q, d).start()
 
     def forward(q):
-        @pl.loop(1, chips)
+        @pl.loop(1, chips, unroll=chips <= 8)
         def _(d):
             ag_copy(q, d).wait_recv()
-            fw_copy(q, d).start()
+
+        fw_copy(q).start()
 
     forward(0)
 
-    @pl.loop(0, chunks)
+    @pl.loop(0, chunks, unroll=4)
     def _(t):
         q = t // per_gather
         j = lax.rem(t, per_gather)
 
         @pl.when(j == 0)
         def _():
-            @pl.loop(0, chips)
-            def _(d):
-                fw_copy(q, d).wait_recv()
+            fw_copy(q).wait_recv()
 
         @pl.when(jnp.logical_and(j == min(1, per_gather - 1), q + 1 < gather_pieces))
         def _():
@@ -298,13 +295,13 @@
         both = part32[p, pl.ds(mine, half)] + from_pair[p].astype(jnp.float32)
         to_chips[p] = both.astype(jnp.bfloat16).reshape(to_chips.shape[1:])
 
-        @pl.loop(1, chips)
+        @pl.loop(1, chips, unroll=chips <= 8)
         def _(d):
             rs_copy(p, d).start()
 
         from_chips[p, chip] = to_chips[p, chip]
 
-    @pl.loop(0, chunks)
+    @pl.loop(0, chunks, unroll=4)
     def _(t):
         p = t // per_sum
         j = lax.rem(t, per_sum)
@@ -333,7 +330,7 @@
     columns = width // sum_pieces
     for p in range(sum_pieces):
 
-        @pl.loop(1, chips)
+        @pl.loop(1, chips, unroll=chips <= 8)
         def _(d):
             rs_copy(p, d).wait_recv()
 
@@ -343,18 +340,17 @@
 
     @pl.loop(0, gather_pieces)
     def _(q):
-        fw_copy(q, 0).wait_send()
-
-        @pl.loop(1, chips)
+        fw_copy(q).wait_send()
+
+        @pl.loop(1, chips, unroll=chips <= 8)
         def _(d):
             ag_copy(q, d).wait_send()
-            fw_copy(q, d).wait_send()
 
     @pl.loop(0, sum_pieces)
     def _(p):
         pair_copy(p).wait_send()
 
-        @pl.loop(1, chips)
+        @pl.loop(1, chips, unroll=chips <= 8)
         def _(d):
             rs_copy(p, d).wait_send()
 
@@ -397,7 +393,7 @@
             pltpu.VMEM(fresh_keys.shape, bf),
             pltpu.VMEM(fresh_values.shape, bf),
             pltpu.VMEM(resid.shape, bf),
-            pltpu.VMEM((1, width), bf),
+            pltpu.VMEM((width,), bf),
             pltpu.VMEM((rows * heads, HEAD_SIZE), f32),
             pltpu.VMEM((rows, width), f32),
             pltpu.VMEM((gu_slots, CHUNK, units), bf),
@@ -418,8 +414,8 @@
             pltpu.SemaphoreType.DMA((dn_slots,)),
             pltpu.SemaphoreType.DMA((gq, chips)),
             pltpu.SemaphoreType.DMA((gq, chips)),
-            pltpu.SemaphoreType.DMA((gq, chips)),
-            pltpu.SemaphoreType.DMA((gq, chips)),
+            pltpu.SemaphoreType.DMA((gq,)),
+            pltpu.SemaphoreType.DMA((gq,)),
             pltpu.SemaphoreType.DMA((sp,)),
             pltpu.SemaphoreType.DMA((sp,)),
             pltpu.SemaphoreType.DMA((sp, chips)),
@@ -442,7 +438,7 @@
         fresh_keys,
         fresh_values,
         resid,
-        gain.reshape(1, width),
+        gain,
         gate_weight,
         up_weight,
         down_weight,

time: 45.3 us -> 42.3 us (0.934)
  Pallas kernels: 42.3 us -> 40.7 us
  local copies, waits for them, and re-layouts: 2.75 us -> 1.4 us
    pallas_call x1, Pallas kernels: 42.3 us -> 40.7 us  [body(): pl.pallas_call(functools.partial(kernel, n, gq, sp), out_shape=jax.ShapeD...]
    reshape x1 -> x0, local copies, waits for them, and re-layouts: 1.35 us -> none  [body(): gain.reshape(1, width)]
where the time goes in v3:
time: 42.3 us; the launch traced here: 42.1 us
  Pallas kernels  40.7 us (96%)
  local copies, waits for them, and re-layouts  1.4 us (3%)
    pallas_call x1, Pallas kernels, body(): pl.pallas_call(functools.partial(kernel, n, gq, sp), out_shape=jax.ShapeD...  40.7 us
    unnamed x1, local copies, waits for them, and re-layouts  1.4 us

profile of v3, /device:TPU:0, one launch (start us, length us, event | category | flops | bytes accessed | tf_op | source)
XLA Modules:
  0.0 42.1 jit_solution(3246575475046267662)
XLA Ops:
  0.0 40.7 %decode_layer.1 = bf16[2,8192]{1,0:T(2,128)(2,1)} custom-call(s32[2]{0:T(128)} %lengths.1, bf16[2,8192]{1,0:T(2,128)(2,1)} %queries.1, bf16[2,256,512]{2,1,0:T(8,128)(2,1)} %keys.1, bf16[2,256,512]{2,1,0:T(8,128)(2,1)} %values.1, bf16[2,512]{1,0:T(2,128)(2,1)} %fresh_keys.1, bf16[2,512]{1,0:T(2,128)(2,1)} %fresh_values.1, bf16[2,8192]{1,0:T(2,128)(2,1)} %resid.1, ...), custom_call_target="tpu_custom_call" | custom-call | flops 2617245696 | bytes 81788928 | tf_op jit(solution)/shard_map/decode_layer/pallas_call | solution.py:384
  40.7 1.4 %copy.13 = bf16[2,8192]{1,0:T(2,128)(2,1)} copy(bf16[2,8192]{1,0:T(2,128)(2,1)} %decode_layer.1) | data formatting | bytes 65536
